TPU v7x, 32 devices: a whole 2x2x4 slice. The times are simulated.
32 devices in a mesh: gy: 8 (over y, x, core), gz: 4 (over z).
Axes of the slice: x: 2, y: 2, z: 4, core: 2. Of those that a mesh axis runs over, the one named last changes fastest.
Arguments:
- volume: bfloat16 [64, 32, 16, 256], P(None, 'gy', 'gz'), may hold values from -2500 to 2500
- down_weight: bfloat16 [128, 64, 2, 2, 2], replicated, may hold values from -0.25 to 0.25
- conv_one: bfloat16 [3, 3, 128, 384], replicated, may hold values from -0.109375 to 0.109375
- conv_two: bfloat16 [3, 3, 128, 384], replicated, may hold values from -0.109375 to 0.109375
- norm_gain: float32 [3, 128], replicated, may hold values from 0.1 to 1.9
- norm_shift: float32 [3, 128], replicated, may hold values from -2.5 to 2.5
Outputs:
- features: bfloat16 [128, 16, 8, 128], P(None, 'gy', 'gz')
All inputs are finite; a program needn't handle non-finite values.
Results may differ from a plain program's by a relative error of at most 0.0065.
Values may be sent and summed in bfloat16 or wider, within the bound.
A program may use at most 64 MiB of HBM per device.

v0:
```python
import jax
import jax.numpy as jnp
from jax import lax
from jax.sharding import PartitionSpec as P


def padded_2(value, sides, width):
    for axis, dim in sides:
        count, length = (lax.axis_size(axis), value.shape[dim])
        up = [(i, (i + 1) % count) for i in range(count - 1)]
        down = [(j, i) for i, j in up]
        last = lax.slice_in_dim(value, length - width, length, axis=dim)
        leading = lax.slice_in_dim(value, 0, width, axis=dim)
        before = lax.ppermute(last, axis, up)
        after = lax.ppermute(leading, axis, down)
        value = jnp.concatenate([before, value, after], axis=dim)
    return value


def leaky(value):
    return jnp.where(value >= 0.0, value, 0.01 * value)


def moments(inner):
    count = float(
        inner.shape[1] * inner.shape[2] * inner.shape[3] * lax.axis_size("gy") * lax.axis_size("gz")
    )
    total, square = lax.psum(
        (jnp.sum(inner, axis=(1, 2, 3)), jnp.sum(inner * inner, axis=(1, 2, 3))), ("gy", "gz")
    )
    mean = total / count
    spread = square / count - mean * mean
    return (mean, spread)


def normalize(value, inner, gain, shift):
    mean, spread = moments(inner)
    scaled = (value - mean[:, None, None, None]) / jnp.sqrt(spread + 1e-05)[:, None, None, None]
    return leaky(scaled * gain[:, None, None, None] + shift[:, None, None, None])


def strided(volume, down_weight):
    blocks = volume.reshape(
        volume.shape[0], volume.shape[1] // 2, 2, volume.shape[2] // 2, 2, volume.shape[3] // 2, 2
    )
    return jnp.einsum(
        "oiabc,iyazbxc->oyzx", down_weight, blocks, preferred_element_type=jnp.float32
    )


def convolve(padded, conv_weight, rows, depth):
    length = padded.shape[3]
    widened = jnp.pad(padded, ((0, 0), (0, 0), (0, 0), (1, 1)))
    stacked = jnp.concatenate(
        [widened[:, :, :, offset : offset + length] for offset in range(3)], axis=0
    )
    total = jnp.zeros((conv_weight.shape[2], rows, depth, length), jnp.float32)
    for row_tap in range(3):
        for depth_tap in range(3):
            piece = stacked[:, row_tap : row_tap + rows, depth_tap : depth_tap + depth, :]
            total = total + jnp.einsum(
                "ok,kyzx->oyzx",
                conv_weight[row_tap, depth_tap],
                piece,
                preferred_element_type=jnp.float32,
            )
    return total


def faces(field):
    return padded_2(field, (("gy", 1), ("gz", 2)), 1)


def on_device(volume, down_weight, conv_one, conv_two, norm_gain, norm_shift):
    coarse = strided(volume, down_weight)
    rows = coarse.shape[1]
    depth = coarse.shape[2]
    first = normalize(coarse, coarse, norm_gain[0], norm_shift[0]).astype(jnp.bfloat16)
    middle = convolve(faces(first), conv_one, rows, depth)
    second = normalize(middle, middle, norm_gain[1], norm_shift[1]).astype(jnp.bfloat16)
    last = convolve(faces(second), conv_two, rows, depth)
    return normalize(last, last, norm_gain[2], norm_shift[2]).astype(jnp.bfloat16)


def solution(mesh):
    return jax.shard_map(
        on_device,
        mesh=mesh,
        in_specs=(P(None, "gy", "gz", None), P(), P(), P(), P(), P()),
        out_specs=P(None, "gy", "gz", None),
        check_vma=False,
    )
```

profile of v0, /device:TPU:0, one launch (start us, length us, event | category | flops | bytes accessed | tf_op | source)
XLA Modules:
  0.0 169.6 jit_solution(1538879256036449937)
XLA Ops:
  0.0 1.7 copy.10
  1.7 0.4 fusion.88
  2.1 42.1 %all-reduce.4 = (f32[128]{0:T(128)S(1)}, f32[128]{0:T(128)S(1)}) all-reduce(f32[128]{0:T(128)S(1)} %get-tuple-element.10, f32[128]{0:T(128)S(1)} %get-tuple-element.9), channel_id=1, replica_groups=mesh['gy'=8,'gz'=4] {'gy','gz'}, use_global_device_ids=true, to_apply=%region_3.0 | all-reduce | flops 256 | bytes 2048 | tf_op jit(solution)/shard_map/psum | solution.py:28
  44.2 0.1 fusion.30
  44.3 1.3 collective-permute-start
  45.6 1.3 collective-permute-start.1
  46.9 4.3 %collective-permute-done.1 = bf16[128,1,2,128]{0,3,2,1:T(8,128)(2,1)S(1)} collective-permute-done((bf16[128,1,2,128]{0,3,2,1:T(8,128)(2,1)S(1)}, bf16[128,1,2,128]{0,3,2,1:T(8,128)(2,1)S(1)}, u32[]{:S(2)}, u32[]{:S(2)}) %collective-permute-start.1) | collective-permute-done | bytes 65568 | tf_op jit(solution)/shard_map/ppermute | solution.py:15
  51.3 3.4 %collective-permute-start.2 = (bf16[128,4,1,128]{0,3,2,1:T(8,128)(2,1)S(1)}, bf16[128,4,1,128]{0,3,2,1:T(8,128)(2,1)S(1)}, u32[]{:S(2)}, u32[]{:S(2)}) collective-permute-start(bf16[128,4,1,128]{0,3,2,1:T(8,128)(2,1)S(1)} %get-tuple-element.23), channel_id=1, source_target_pairs={{0,1},{1,2},{2,3},{4,5},{5,6},{6,7},{8,9},{9,10},{10,11},{12,13},{... | collective-permute-start | bytes 393224 | tf_op jit(solution)/shard_map/ppermute | solution.py:14
  54.7 1.3 collective-permute-start.3
  56.0 1.2 collective-permute-done.2
  57.2 4.4 %collective-permute-done.3 = bf16[128,4,1,128]{0,3,2,1:T(8,128)(2,1)S(1)} collective-permute-done((bf16[128,4,1,128]{0,3,2,1:T(8,128)(2,1)S(1)}, bf16[128,4,1,128]{0,3,2,1:T(8,128)(2,1)S(1)}, u32[]{:S(2)}, u32[]{:S(2)}) %collective-permute-start.3) | collective-permute-done | bytes 131104 | tf_op jit(solution)/shard_map/ppermute | solution.py:15
  61.6 0.2 fusion.25
  61.8 0.3 fusion.90
  62.0 0.2 pad_maximum_fusion
  62.3 0.9 copy-done
  63.2 0.3 fusion.51
  63.5 0.3 fusion.53
  63.7 0.3 fusion.55
  64.0 0.3 fusion.57
  64.3 0.3 fusion.59
  64.6 0.3 fusion.61
  64.8 0.3 fusion.63
  65.1 0.3 fusion.65
  65.4 0.3 fusion.87
  65.7 41.1 %all-reduce.3 = (f32[128]{0:T(128)S(1)}, f32[128]{0:T(128)S(1)}) all-reduce(f32[128]{0:T(128)S(1)} %get-tuple-element.8, f32[128]{0:T(128)S(1)} %get-tuple-element.7), channel_id=1, replica_groups=mesh['gy'=8,'gz'=4] {'gy','gz'}, use_global_device_ids=true, to_apply=%region_7.8 | all-reduce | flops 256 | bytes 2048 | tf_op jit(solution)/shard_map/psum | solution.py:28
  106.8 0.1 fusion.31
  106.9 1.3 collective-permute-start.4
  108.2 1.3 collective-permute-start.5
  109.6 4.3 %collective-permute-done.5 = bf16[128,1,2,128]{0,3,2,1:T(8,128)(2,1)S(1)} collective-permute-done((bf16[128,1,2,128]{0,3,2,1:T(8,128)(2,1)S(1)}, bf16[128,1,2,128]{0,3,2,1:T(8,128)(2,1)S(1)}, u32[]{:S(2)}, u32[]{:S(2)}) %collective-permute-start.5) | collective-permute-done | bytes 65568 | tf_op jit(solution)/shard_map/ppermute | solution.py:15
  114.0 2.5 %collective-permute-start.6 = (bf16[128,4,1,128]{0,3,2,1:T(8,128)(2,1)S(1)}, bf16[128,4,1,128]{0,3,2,1:T(8,128)(2,1)S(1)}, u32[]{:S(2)}, u32[]{:S(2)}) collective-permute-start(bf16[128,4,1,128]{0,3,2,1:T(8,128)(2,1)S(1)} %get-tuple-element.21), channel_id=1, source_target_pairs={{0,1},{1,2},{2,3},{4,5},{5,6},{6,7},{8,9},{9,10},{10,11},{12,13},{... | collective-permute-start | bytes 393224 | tf_op jit(solution)/shard_map/ppermute | solution.py:14
  116.5 1.3 collective-permute-start.7
  117.8 1.2 collective-permute-done.6
  119.0 4.4 %collective-permute-done.7 = bf16[128,4,1,128]{0,3,2,1:T(8,128)(2,1)S(1)} collective-permute-done((bf16[128,4,1,128]{0,3,2,1:T(8,128)(2,1)S(1)}, bf16[128,4,1,128]{0,3,2,1:T(8,128)(2,1)S(1)}, u32[]{:S(2)}, u32[]{:S(2)}) %collective-permute-start.7) | collective-permute-done | bytes 131104 | tf_op jit(solution)/shard_map/ppermute | solution.py:15
  123.3 0.2 select_maximum_fusion
  123.5 0.3 fusion.89
  123.8 0.2 pad_maximum_fusion.1
  124.1 0.9 copy-done.1
  125.0 0.3 fusion.34
  125.2 0.3 fusion.36
  125.5 0.3 fusion.38
  125.8 0.3 fusion.40
  126.0 0.3 fusion.42
  126.3 0.3 fusion.44
  126.6 0.3 fusion.46
  126.9 0.3 fusion.48
  127.1 0.3 fusion.86
  127.5 41.2 %all-reduce.2 = (f32[128]{0:T(128)S(1)}, f32[128]{0:T(128)S(1)}) all-reduce(f32[128]{0:T(128)S(1)} %get-tuple-element.6, f32[128]{0:T(128)S(1)} %get-tuple-element.5), channel_id=1, replica_groups=mesh['gy'=8,'gz'=4] {'gy','gz'}, use_global_device_ids=true, to_apply=%region_11.12 | all-reduce | flops 256 | bytes 2048 | tf_op jit(solution)/shard_map/psum | solution.py:28
  168.8 0.8 copy.13
  (21 shorter events, 0.3 us)
Async XLA Ops:
  0.0 1.7 copy-start.2
  0.0 1.7 copy-start.3
  0.0 1.7 %copy-start.4 = (bf16[128,64,2,2,2]{0,4,3,2,1:T(2,128)(2,1)S(1)}, bf16[128,64,2,2,2]{0,4,3,2,1:T(2,128)(2,1)}, u32[]{:S(2)}) copy-start(bf16[128,64,2,2,2]{0,4,3,2,1:T(2,128)(2,1)} %param.7) | copy-start | bytes 393220
  44.3 2.6 %collective-permute-start = (bf16[128,1,2,128]{0,3,2,1:T(8,128)(2,1)S(1)}, bf16[128,1,2,128]{0,3,2,1:T(8,128)(2,1)S(1)}, u32[]{:S(2)}, u32[]{:S(2)}) collective-permute-start(bf16[128,1,2,128]{0,3,2,1:T(8,128)(2,1)S(1)} %get-tuple-element.27), channel_id=1, source_target_pairs={{0,4},{4,8},{8,12},{12,16},{16,20},{20,24},{24,28},{1,5},{5,9},{9,... | collective-permute-start | bytes 196616 | tf_op jit(solution)/shard_map/ppermute | solution.py:14
  45.6 5.7 %collective-permute-start.1 = (bf16[128,1,2,128]{0,3,2,1:T(8,128)(2,1)S(1)}, bf16[128,1,2,128]{0,3,2,1:T(8,128)(2,1)S(1)}, u32[]{:S(2)}, u32[]{:S(2)}) collective-permute-start(bf16[128,1,2,128]{0,3,2,1:T(8,128)(2,1)S(1)} %get-tuple-element.28), channel_id=1, source_target_pairs={{4,0},{8,4},{12,8},{16,12},{20,16},{24,20},{28,24},{5,1},{9,5},{13... | collective-permute-start | bytes 196616 | tf_op jit(solution)/shard_map/ppermute | solution.py:15
  51.3 5.9 %collective-permute-start.2 = (bf16[128,4,1,128]{0,3,2,1:T(8,128)(2,1)S(1)}, bf16[128,4,1,128]{0,3,2,1:T(8,128)(2,1)S(1)}, u32[]{:S(2)}, u32[]{:S(2)}) collective-permute-start(bf16[128,4,1,128]{0,3,2,1:T(8,128)(2,1)S(1)} %get-tuple-element.23), channel_id=1, source_target_pairs={{0,1},{1,2},{2,3},{4,5},{5,6},{6,7},{8,9},{9,10},{10,11},{12,13},{... | collective-permute-start | bytes 393224 | tf_op jit(solution)/shard_map/ppermute | solution.py:14
  54.7 6.9 %collective-permute-start.3 = (bf16[128,4,1,128]{0,3,2,1:T(8,128)(2,1)S(1)}, bf16[128,4,1,128]{0,3,2,1:T(8,128)(2,1)S(1)}, u32[]{:S(2)}, u32[]{:S(2)}) collective-permute-start(bf16[128,4,1,128]{0,3,2,1:T(8,128)(2,1)S(1)} %get-tuple-element.24), channel_id=1, source_target_pairs={{1,0},{2,1},{3,2},{5,4},{6,5},{7,6},{9,8},{10,9},{11,10},{13,12},{... | collective-permute-start | bytes 393224 | tf_op jit(solution)/shard_map/ppermute | solution.py:15
  62.0 1.2 copy-start
  106.9 2.6 %collective-permute-start.4 = (bf16[128,1,2,128]{0,3,2,1:T(8,128)(2,1)S(1)}, bf16[128,1,2,128]{0,3,2,1:T(8,128)(2,1)S(1)}, u32[]{:S(2)}, u32[]{:S(2)}) collective-permute-start(bf16[128,1,2,128]{0,3,2,1:T(8,128)(2,1)S(1)} %get-tuple-element.25), channel_id=1, source_target_pairs={{0,4},{4,8},{8,12},{12,16},{16,20},{20,24},{24,28},{1,5},{5,9},{9,... | collective-permute-start | bytes 196616 | tf_op jit(solution)/shard_map/ppermute | solution.py:14
  108.2 5.7 %collective-permute-start.5 = (bf16[128,1,2,128]{0,3,2,1:T(8,128)(2,1)S(1)}, bf16[128,1,2,128]{0,3,2,1:T(8,128)(2,1)S(1)}, u32[]{:S(2)}, u32[]{:S(2)}) collective-permute-start(bf16[128,1,2,128]{0,3,2,1:T(8,128)(2,1)S(1)} %get-tuple-element.26), channel_id=1, source_target_pairs={{4,0},{8,4},{12,8},{16,12},{20,16},{24,20},{28,24},{5,1},{9,5},{13... | collective-permute-start | bytes 196616 | tf_op jit(solution)/shard_map/ppermute | solution.py:15
  114.0 5.0 %collective-permute-start.6 = (bf16[128,4,1,128]{0,3,2,1:T(8,128)(2,1)S(1)}, bf16[128,4,1,128]{0,3,2,1:T(8,128)(2,1)S(1)}, u32[]{:S(2)}, u32[]{:S(2)}) collective-permute-start(bf16[128,4,1,128]{0,3,2,1:T(8,128)(2,1)S(1)} %get-tuple-element.21), channel_id=1, source_target_pairs={{0,1},{1,2},{2,3},{4,5},{5,6},{6,7},{8,9},{9,10},{10,11},{12,13},{... | collective-permute-start | bytes 393224 | tf_op jit(solution)/shard_map/ppermute | solution.py:14
  116.5 6.9 %collective-permute-start.7 = (bf16[128,4,1,128]{0,3,2,1:T(8,128)(2,1)S(1)}, bf16[128,4,1,128]{0,3,2,1:T(8,128)(2,1)S(1)}, u32[]{:S(2)}, u32[]{:S(2)}) collective-permute-start(bf16[128,4,1,128]{0,3,2,1:T(8,128)(2,1)S(1)} %get-tuple-element.22), channel_id=1, source_target_pairs={{1,0},{2,1},{3,2},{5,4},{6,5},{7,6},{9,8},{10,9},{11,10},{13,12},{... | collective-permute-start | bytes 393224 | tf_op jit(solution)/shard_map/ppermute | solution.py:15
  123.8 1.2 copy-start.1
where the time goes:
time: 170 us
  blocking collectives  124 us (73%)
  waiting for transfers between devices  19.8 us (12%)
  starting transfers between devices  13.7 us (8%)
  matrix products  5.24 us (3%)
  local copies, waits for them, and re-layouts  4.9 us (3%)
    psum x3, blocking collectives, moments(): lax.psum((jnp.sum(inner, axis=(1, 2, 3)), jnp.sum(inner * inner, axis=(1,...  124 us
    ppermute x4, waiting for transfers between devices, padded_2(): after = lax.ppermute(leading, axis, down)  17.4 us
    ppermute x4, starting transfers between devices, padded_2(): before = lax.ppermute(last, axis, up)  8.52 us
    ppermute x4, starting transfers between devices, padded_2(): after = lax.ppermute(leading, axis, down)  5.17 us
    dot_general x18, matrix products, convolve(): jnp.einsum('ok,kyzx->oyzx', conv_weight[row_tap, depth_tap], piece, prefe...  4.86 us
    unnamed x11, local copies, waits for them, and re-layouts  3.49 us
  transfers between devices with their start and end apart: 8, of which 6 were waited for; matrix products, arithmetic and copies ran while one was open for 0% of the time, Pallas kernels for 0%

commit v1 on v0

v1 whole, which is shorter than its diff:
```python
import functools

import jax
import jax.numpy as jnp
from jax import lax
from jax.experimental import pallas as pl
from jax.experimental.pallas import tpu as pltpu
from jax.sharding import PartitionSpec as P

MESH = pl.DeviceIdType.MESH
SIDES = [(dy, dz) for dy in (-1, 0, 1) for dz in (-1, 0, 1) if (dy, dz) != (0, 0)]


def strided(volume, down_weight):
    blocks = volume.reshape(
        volume.shape[0], volume.shape[1] // 2, 2, volume.shape[2] // 2, 2, volume.shape[3] // 2, 2
    )
    return jnp.einsum(
        "oiabc,iyazbxc->yzxo", down_weight, blocks, preferred_element_type=jnp.float32
    )


def kernel(
    ny, nz,
    coarse_ref, one_hbm, two_hbm, gain_ref, shift_ref, out_ref,
    one_ref, two_ref, stat_out, stat_in, rim_out, rim_in, field,
    load_sem, stat_send, stat_recv, rim_send, rim_recv,
):
    count = ny * nz
    my, mz = lax.axis_index("gy"), lax.axis_index("gz")
    me = my * nz + mz
    rows, depth, length, channels = coarse_ref.shape
    cells = rows * depth * length

    loads = [
        pltpu.make_async_copy(one_hbm, one_ref, load_sem.at[0]),
        pltpu.make_async_copy(two_hbm, two_ref, load_sem.at[1]),
    ]
    for load in loads:
        load.start()

    def device(k):
        flat = lax.rem(me + k, count)
        return (flat // nz, lax.rem(flat, nz))

    barrier = pltpu.get_barrier_semaphore()

    def greet(k, _):
        pl.semaphore_signal(barrier, inc=1, device_id=device(k), device_id_type=MESH)
        return 0

    lax.fori_loop(1, count, greet, 0)
    pl.semaphore_wait(barrier, count - 1)

    def present(side):
        y, z = my + side[0], mz + side[1]
        return (y >= 0) & (y < ny) & (z >= 0) & (z < nz)

    def outer(d, n):
        return {-1: slice(0, 1), 0: slice(1, n + 1), 1: slice(n + 1, n + 2)}[d]

    def inner(d, n):
        return {-1: slice(0, 1), 0: slice(0, n), 1: slice(n - 1, n)}[d]

    def rim_copy(turn, s):
        dy, dz = SIDES[s]
        opposite = len(SIDES) - 1 - s
        return pltpu.make_async_remote_copy(
            src_ref=rim_out.at[turn, inner(dy, rows), inner(dz, depth)],
            dst_ref=rim_in.at[turn, outer(-dy, rows), outer(-dz, depth)],
            send_sem=rim_send.at[turn, s],
            recv_sem=rim_recv.at[turn, opposite],
            device_id=(my + dy, mz + dz),
            device_id_type=MESH,
        )

    def rim_arrival(turn, s):
        dy, dz = SIDES[s]
        slot = rim_in.at[turn, outer(dy, rows), outer(dz, depth)]
        return pltpu.make_async_remote_copy(
            src_ref=slot, dst_ref=slot,
            send_sem=rim_send.at[turn, s], recv_sem=rim_recv.at[turn, s],
            device_id=(my, mz), device_id_type=MESH,
        )

    def stat_all(turn):
        block = stat_in.at[turn, pl.ds(0, count - 1)]
        return pltpu.make_async_remote_copy(
            src_ref=block, dst_ref=block,
            send_sem=stat_send.at[turn], recv_sem=stat_recv.at[turn],
            device_id=(my, mz), device_id_type=MESH,
        )

    def send(turn, value):
        mean = jnp.sum(value, axis=0, keepdims=True) / cells
        centred = value - mean
        spread = jnp.sum(centred * centred, axis=0, keepdims=True)
        stat_out[turn] = jnp.concatenate([mean, spread], axis=0)

        def push(k, _):
            pltpu.make_async_remote_copy(
                src_ref=stat_out.at[turn],
                dst_ref=stat_in.at[turn, k - 1],
                send_sem=stat_send.at[turn],
                recv_sem=stat_recv.at[turn],
                device_id=device(k),
                device_id_type=MESH,
            ).start()
            return 0

        lax.fori_loop(1, count, push, 0)
        if turn < 2:
            rim_out[turn] = centred.astype(jnp.bfloat16).reshape(rows, depth, length, channels)
            for s in range(len(SIDES)):
                @pl.when(present(SIDES[s]))
                def _():
                    rim_copy(turn, s).start()
        return mean, spread

    def leaky(value):
        return jnp.where(value >= 0.0, value, 0.01 * value)

    def finish(turn, mean, spread):
        stat_all(turn).wait_recv()
        others = stat_in[turn]
        centre = (jnp.sum(others[:, 0:1, :], axis=0) + mean) / count
        offsets = others[:, 0:1, :] - centre
        total = jnp.sum(others[:, 1:2, :] + cells * (offsets * offsets), axis=0)
        total = total + spread + cells * ((mean - centre) * (mean - centre))
        scale = gain_ref[turn:turn + 1] * lax.rsqrt(total / (cells * count) + 1e-5)
        return centre, scale, shift_ref[turn:turn + 1], others

    def normalized_field(turn, value, mean, spread):
        centre, scale, shift, others = finish(turn, mean, spread)
        own = leaky((value - centre) * scale + shift).astype(jnp.bfloat16)
        field[1:rows + 1, 1:depth + 1] = own.reshape(rows, depth, length, channels)
        for s, (dy, dz) in enumerate(SIDES):
            ok = present((dy, dz))

            @pl.when(ok)
            def _():
                rim_arrival(turn, s).wait_recv()
                origin = (-(dy * nz + dz)) % count
                bias = others[origin - 1, 0:1, :] - centre
                raw = rim_in[turn, outer(dy, rows), outer(dz, depth)].astype(jnp.float32)
                field[outer(dy, rows), outer(dz, depth)] = leaky(
                    (raw + bias) * scale + shift
                ).astype(jnp.bfloat16)

            @pl.when(jnp.logical_not(ok))
            def _():
                slot = field.at[outer(dy, rows), outer(dz, depth)]
                slot[...] = jnp.zeros(slot.shape, jnp.bfloat16)

    def convolve(weight):
        left = jnp.concatenate(
            [
                field[p:p + rows, q:q + depth].reshape(cells, channels)
                for p in range(3) for q in range(3)
            ],
            axis=1,
        )
        parts = []
        for r in range(3):
            right = jnp.concatenate(
                [
                    weight[p, q, :, r * channels:(r + 1) * channels]
                    for p in range(3) for q in range(3)
                ],
                axis=1,
            )
            parts.append(
                lax.dot_general(
                    left, right, (((1,), (1,)), ((), ())), preferred_element_type=jnp.float32
                )
            )
        place = lax.rem(lax.broadcasted_iota(jnp.int32, (cells, channels), 0), length)
        before = jnp.where(place == 0, 0.0, pltpu.roll(parts[0], 1, 0))
        after = jnp.where(place == length - 1, 0.0, pltpu.roll(parts[2], cells - 1, 0))
        return parts[1] + before + after

    value = coarse_ref[...].reshape(cells, channels)
    for turn, weight in enumerate((one_ref, two_ref)):
        mean, spread = send(turn, value)
        normalized_field(turn, value, mean, spread)
        loads[turn].wait()
        value = convolve(weight)
    mean, spread = send(2, value)
    centre, scale, shift, _ = finish(2, mean, spread)
    out = leaky((value - centre) * scale + shift).astype(jnp.bfloat16)
    out_ref[...] = out.reshape(rows, depth, length, channels)

    for turn in range(3):
        stat_all(turn).wait_send()
        if turn < 2:
            for s in range(len(SIDES)):
                @pl.when(present(SIDES[s]))
                def _():
                    rim_copy(turn, s).wait_send()


def on_device(ny, nz, volume, down_weight, conv_one, conv_two, norm_gain, norm_shift):
    coarse = strided(volume, down_weight)
    rows, depth, length, channels = coarse.shape
    vmem = pl.BlockSpec(memory_space=pltpu.VMEM)
    hbm = pl.BlockSpec(memory_space=pl.ANY)
    count = ny * nz
    out = pl.pallas_call(
        functools.partial(kernel, ny, nz),
        out_shape=jax.ShapeDtypeStruct(coarse.shape, jnp.bfloat16),
        in_specs=[vmem, hbm, hbm, vmem, vmem],
        out_specs=vmem,
        scratch_shapes=[
            pltpu.VMEM(conv_one.shape, jnp.bfloat16),
            pltpu.VMEM(conv_two.shape, jnp.bfloat16),
            pltpu.VMEM((3, 2, channels), jnp.float32),
            pltpu.VMEM((3, count - 1, 2, channels), jnp.float32),
            pltpu.VMEM((2, rows, depth, length, channels), jnp.bfloat16),
            pltpu.VMEM((2, rows + 2, depth + 2, length, channels), jnp.bfloat16),
            pltpu.VMEM((rows + 2, depth + 2, length, channels), jnp.bfloat16),
            pltpu.SemaphoreType.DMA((2,)),
            pltpu.SemaphoreType.DMA((3,)),
            pltpu.SemaphoreType.DMA((3,)),
            pltpu.SemaphoreType.DMA((2, len(SIDES))),
            pltpu.SemaphoreType.DMA((2, len(SIDES))),
        ],
        compiler_params=pltpu.CompilerParams(
            collective_id=0, has_side_effects=True, vmem_limit_bytes=40 * 1024 * 1024
        ),
    )(coarse, conv_one, conv_two, norm_gain, norm_shift)
    return jnp.transpose(out, (3, 0, 1, 2))


def solution(mesh):
    return jax.shard_map(
        functools.partial(on_device, mesh.shape["gy"], mesh.shape["gz"]),
        mesh=mesh,
        in_specs=(P(None, "gy", "gz", None), P(), P(), P(), P(), P()),
        out_specs=P(None, "gy", "gz", None),
        check_vma=False,
    )
```

time: 170 us -> 32.1 us (0.19)
  blocking collectives: 124 us -> 0 us
  Pallas kernels: 0 us -> 27.2 us
  waiting for transfers between devices: 19.8 us -> 0 us
  starting transfers between devices: 13.7 us -> 0 us
  matrix products: 5.24 us -> 0.35 us
    psum x3 -> x0, blocking collectives: 124 us -> none  [moments(): lax.psum((jnp.sum(inner, axis=(1, 2, 3)), jnp.sum(inner * inner, axis=(1,...]
    pallas_call x0 -> x1, Pallas kernels: none -> 27.2 us  [on_device(): pl.pallas_call(functools.partial(kernel, ny, nz), out_shape=jax.ShapeDtyp...]
    ppermute x8 -> x0, waiting for transfers between devices: 19.8 us -> none  [the longest x4 17.4 us: padded_2(): after = lax.ppermute(leading, axis, down)]
    ppermute x8 -> x0, starting transfers between devices: 13.7 us -> none  [the longest x4 8.52 us: padded_2(): before = lax.ppermute(last, axis, up)]
    dot_general x19 -> x1, matrix products: 5.24 us -> 0.35 us  [strided(): jnp.einsum('oiabc,iyazbxc->yzxo', down_weight, blocks, preferred_element_...]
  transfers between devices with their start and end apart: 8 -> 0, of which waited for: 6 -> 0; matrix products, arithmetic and copies ran while one was open for 0% -> 0% of each run, Pallas kernels for 0% -> 0%
where the time goes in v1:
time: 32.1 us; the launch traced here: 31.9 us
  Pallas kernels  27.2 us (85%)
  local copies, waits for them, and re-layouts  4.36 us (14%)
  matrix products  0.35 us (1%)
    pallas_call x1, Pallas kernels, on_device(): pl.pallas_call(functools.partial(kernel, ny, nz), out_shape=jax.ShapeDtyp...  27.2 us
    unnamed x11, local copies, waits for them, and re-layouts  3.57 us
    transpose x1, local copies, waits for them, and re-layouts, on_device(): return jnp.transpose(out, (3, 0, 1, 2))  0.79 us

profile of v1, /device:TPU:0, one launch (start us, length us, event | category | flops | bytes accessed | tf_op | source)
XLA Modules:
  0.0 31.9 jit_solution(3151166753113064023)
XLA Ops:
  0.0 0.0 copy-start
  0.0 0.9 %copy-done = bf16[128,64,2,2,2]{0,4,3,2,1:T(2,128)(2,1)S(1)} copy-done((bf16[128,64,2,2,2]{0,4,3,2,1:T(2,128)(2,1)S(1)}, bf16[128,64,2,2,2]{0,4,3,2,1:T(2,128)(2,1)}, u32[]{:S(2)}) %copy-start) | copy-done | bytes 131096
  0.9 1.6 %copy.10 = bf16[64,4,4,256]{0,3,2,1:T(8,128)(2,1)S(1)} copy(bf16[64,4,4,256]{3,2,1,0:T(4,128)(2,1)} %param.6) | data formatting | bytes 1048576 | tf_op args[0]
  2.5 0.0 copy-start.1
  2.5 0.0 copy-start.2
  2.6 0.0 copy-start.3
  2.6 0.0 copy-start.4
  2.6 0.4 %convolution_bitcast_fusion.coarse_ref = f32[2,2,128,128]{3,2,1,0:T(8,128)S(1)} fusion(bf16[64,2,2,2,2,128,2]{0,6,5,4,3,2,1:T(2,128)(2,1)S(1)} %bitcast.9, bf16[128,64,2,2,2,1,1]{0,4,3,2,1,6,5:T(2,128)(2,1)S(1)} %bitcast.7), kind=kOutput, calls=%fused_computation | convolution fusion | flops 67108864 | bytes 917504 | tf_op jit(solution)/shard_map/oiabc,iyazbxc->yzxo/dot_general | solution.py:18
  2.9 0.8 %copy-done.1 = bf16[3,3,128,384]{3,2,1,0:T(8,128)(2,1)S(1)} copy-done((bf16[3,3,128,384]{3,2,1,0:T(8,128)(2,1)S(1)}, bf16[3,3,128,384]{3,2,1,0:T(8,128)(2,1)}, u32[]{:S(2)}) %copy-start.1) | copy-done | bytes 884760
  3.7 0.3 copy-done.2
  4.0 0.0 copy-done.3
  4.0 0.0 copy-done.4
  4.0 27.2 %shard_map.64 = bf16[2,2,128,128]{3,2,1,0:T(8,128)(2,1)S(1)} custom-call(f32[2,2,128,128]{3,2,1,0:T(8,128)S(1)} %convolution_bitcast_fusion.coarse_ref, bf16[3,3,128,384]{3,2,1,0:T(8,128)(2,1)S(1)} %copy-done.1, bf16[3,3,128,384]{3,2,1,0:T(8,128)(2,1)S(1)} %copy-done.2, f32[3,128]{1,0:T(4,128)S(1)} %copy-done.3, f32[3,128]{1,0:T(4,128)S(1)} %copy-done.4), custom_call_target="tpu_custom_call" | custom-call | tf_op jit(solution)/shard_map/pallas_call | solution.py:208
  31.2 0.8 %copy.13 = bf16[128,2,2,128]{3,2,1,0:T(2,128)(2,1)} copy(bf16[128,2,2,128]{0,3,2,1:T(8,128)(2,1)S(1)} %bitcast.8) | data formatting | bytes 262144 | tf_op jit(solution)/shard_map/transpose | solution.py:231
Async XLA Ops:
  0.0 0.9 %copy-start = (bf16[128,64,2,2,2]{0,4,3,2,1:T(2,128)(2,1)S(1)}, bf16[128,64,2,2,2]{0,4,3,2,1:T(2,128)(2,1)}, u32[]{:S(2)}) copy-start(bf16[128,64,2,2,2]{0,4,3,2,1:T(2,128)(2,1)} %param.7) | copy-start | bytes 393220
  2.5 1.2 %copy-start.1 = (bf16[3,3,128,384]{3,2,1,0:T(8,128)(2,1)S(1)}, bf16[3,3,128,384]{3,2,1,0:T(8,128)(2,1)}, u32[]{:S(2)}) copy-start(bf16[3,3,128,384]{3,2,1,0:T(8,128)(2,1)} %one_hbm.1) | copy-start | bytes 2654212
  2.5 1.4 %copy-start.2 = (bf16[3,3,128,384]{3,2,1,0:T(8,128)(2,1)S(1)}, bf16[3,3,128,384]{3,2,1,0:T(8,128)(2,1)}, u32[]{:S(2)}) copy-start(bf16[3,3,128,384]{3,2,1,0:T(8,128)(2,1)} %two_hbm.1) | copy-start | bytes 2654212
  2.6 1.4 %copy-start.3 = (f32[3,128]{1,0:T(4,128)S(1)}, f32[3,128]{1,0:T(4,128)}, u32[]{:S(2)}) copy-start(f32[3,128]{1,0:T(4,128)} %gain_ref.1) | copy-start | bytes 4612
  2.6 1.4 %copy-start.4 = (f32[3,128]{1,0:T(4,128)S(1)}, f32[3,128]{1,0:T(4,128)}, u32[]{:S(2)}) copy-start(f32[3,128]{1,0:T(4,128)} %shift_ref.1) | copy-start | bytes 4612

commit v2 on v1

--- a/solution.py
+++ b/solution.py
@@ -11,46 +11,46 @@
 SIDES = [(dy, dz) for dy in (-1, 0, 1) for dz in (-1, 0, 1) if (dy, dz) != (0, 0)]
 
 
-def strided(volume, down_weight):
-    blocks = volume.reshape(
-        volume.shape[0], volume.shape[1] // 2, 2, volume.shape[2] // 2, 2, volume.shape[3] // 2, 2
-    )
-    return jnp.einsum(
-        "oiabc,iyazbxc->yzxo", down_weight, blocks, preferred_element_type=jnp.float32
-    )
-
-
 def kernel(
     ny, nz,
-    coarse_ref, one_hbm, two_hbm, gain_ref, shift_ref, out_ref,
-    one_ref, two_ref, stat_out, stat_in, rim_out, rim_in, field,
+    volume_hbm, down_hbm, one_hbm, two_hbm, gain_ref, shift_ref, out_ref,
+    volume_ref, down_ref, wide, taps, pairs, one_ref, two_ref, right, stat_out, stat_in, rim_out, rim_in, field,
     load_sem, stat_send, stat_recv, rim_send, rim_recv,
 ):
     count = ny * nz
     my, mz = lax.axis_index("gy"), lax.axis_index("gz")
     me = my * nz + mz
-    rows, depth, length, channels = coarse_ref.shape
+    rows, depth, length, channels = out_ref.shape
+    inputs = volume_ref.shape[0]
     cells = rows * depth * length
 
     loads = [
-        pltpu.make_async_copy(one_hbm, one_ref, load_sem.at[0]),
-        pltpu.make_async_copy(two_hbm, two_ref, load_sem.at[1]),
+        pltpu.make_async_copy(volume_hbm, volume_ref, load_sem.at[0]),
+        pltpu.make_async_copy(down_hbm, down_ref, load_sem.at[1]),
+        pltpu.make_async_copy(one_hbm, one_ref, load_sem.at[2]),
+        pltpu.make_async_copy(two_hbm, two_ref, load_sem.at[3]),
     ]
     for load in loads:
         load.start()
 
-    def device(k):
-        flat = lax.rem(me + k, count)
-        return (flat // nz, lax.rem(flat, nz))
+    def device(dy, dz):
+        y, z = my + dy, mz + dz
+        return (jnp.where(y >= ny, y - ny, y), jnp.where(z >= nz, z - nz, z))
+    def peers(act):
+        for dz in range(1, nz):
+            act(0, dz)
+        def body(dy, _):
+            for dz in range(nz):
+                act(dy, dz)
+            return 0
+        lax.fori_loop(1, ny, body, 0, unroll=True)
 
     barrier = pltpu.get_barrier_semaphore()
 
-    def greet(k, _):
-        pl.semaphore_signal(barrier, inc=1, device_id=device(k), device_id_type=MESH)
-        return 0
-
-    lax.fori_loop(1, count, greet, 0)
-    pl.semaphore_wait(barrier, count - 1)
+    def greet(dy, dz):
+        pl.semaphore_signal(barrier, inc=1, device_id=device(dy, dz), device_id_type=MESH)
+
+    peers(greet)
 
     def present(side):
         y, z = my + side[0], mz + side[1]
@@ -97,18 +97,17 @@
         spread = jnp.sum(centred * centred, axis=0, keepdims=True)
         stat_out[turn] = jnp.concatenate([mean, spread], axis=0)
 
-        def push(k, _):
+        def push(dy, dz):
             pltpu.make_async_remote_copy(
                 src_ref=stat_out.at[turn],
-                dst_ref=stat_in.at[turn, k - 1],
+                dst_ref=stat_in.at[turn, dy * nz + dz - 1],
                 send_sem=stat_send.at[turn],
                 recv_sem=stat_recv.at[turn],
-                device_id=device(k),
+                device_id=device(dy, dz),
                 device_id_type=MESH,
             ).start()
-            return 0
-
-        lax.fori_loop(1, count, push, 0)
+
+        peers(push)
         if turn < 2:
             rim_out[turn] = centred.astype(jnp.bfloat16).reshape(rows, depth, length, channels)
             for s in range(len(SIDES)):
@@ -140,7 +139,7 @@
             @pl.when(ok)
             def _():
                 rim_arrival(turn, s).wait_recv()
-                origin = (-(dy * nz + dz)) % count
+                origin = (-dy % ny) * nz + (-dz % nz)
                 bias = others[origin - 1, 0:1, :] - centre
                 raw = rim_in[turn, outer(dy, rows), outer(dz, depth)].astype(jnp.float32)
                 field[outer(dy, rows), outer(dz, depth)] = leaky(
@@ -152,7 +151,49 @@
                 slot = field.at[outer(dy, rows), outer(dz, depth)]
                 slot[...] = jnp.zeros(slot.shape, jnp.bfloat16)
 
-    def convolve(weight):
+    def strided():
+        loads[1].wait()
+        taps[...] = down_ref[...].astype(jnp.float32)
+        factor = jnp.concatenate(
+            [
+                jnp.concatenate(
+                    [taps[pl.ds(4 * a + 2 * b + c, inputs, stride=8)] for a in range(2) for b in range(2)],
+                    axis=0,
+                )
+                for c in range(2)
+            ],
+            axis=1,
+        ).astype(jnp.bfloat16)
+        loads[0].wait()
+        wide[...] = volume_ref[...].astype(jnp.float32)
+        made = []
+        for y in range(rows):
+            for z in range(depth):
+                block = jnp.concatenate(
+                    [wide[:, 2 * y + a, 2 * z + b] for a in range(2) for b in range(2)], axis=0
+                ).astype(jnp.bfloat16)
+                both = lax.dot_general(
+                    block, factor, (((0,), (0,)), ((), ())), preferred_element_type=jnp.float32
+                )
+                start = (y * depth + z) * 2 * length
+                made.append(0.0)
+                for c in range(2):
+                    pairs[c, start:start + 2 * length] = both[:, c * channels:(c + 1) * channels]
+                    made[-1] += pairs[c, pl.ds(start + c, length, stride=2)]
+        return jnp.concatenate(made, axis=0)
+
+    def arrange(weight):
+        right[...] = jnp.concatenate(
+            [
+                jnp.concatenate(
+                    [weight[p, q, :, r * channels:(r + 1) * channels].T for r in range(3)], axis=1
+                )
+                for p in range(3) for q in range(3)
+            ],
+            axis=0,
+        )
+
+    def convolve():
         left = jnp.concatenate(
             [
                 field[p:p + rows, q:q + depth].reshape(cells, channels)
@@ -160,31 +201,21 @@
             ],
             axis=1,
         )
-        parts = []
-        for r in range(3):
-            right = jnp.concatenate(
-                [
-                    weight[p, q, :, r * channels:(r + 1) * channels]
-                    for p in range(3) for q in range(3)
-                ],
-                axis=1,
-            )
-            parts.append(
-                lax.dot_general(
-                    left, right, (((1,), (1,)), ((), ())), preferred_element_type=jnp.float32
-                )
-            )
+        product = jnp.dot(left, right[...], preferred_element_type=jnp.float32)
+        parts = [product[:, r * channels:(r + 1) * channels] for r in range(3)]
         place = lax.rem(lax.broadcasted_iota(jnp.int32, (cells, channels), 0), length)
         before = jnp.where(place == 0, 0.0, pltpu.roll(parts[0], 1, 0))
         after = jnp.where(place == length - 1, 0.0, pltpu.roll(parts[2], cells - 1, 0))
         return parts[1] + before + after
 
-    value = coarse_ref[...].reshape(cells, channels)
+    value = strided()
+    pl.semaphore_wait(barrier, count - 1)
     for turn, weight in enumerate((one_ref, two_ref)):
         mean, spread = send(turn, value)
+        loads[2 + turn].wait()
+        arrange(weight)
         normalized_field(turn, value, mean, spread)
-        loads[turn].wait()
-        value = convolve(weight)
+        value = convolve()
     mean, spread = send(2, value)
     centre, scale, shift, _ = finish(2, mean, spread)
     out = leaky((value - centre) * scale + shift).astype(jnp.bfloat16)
@@ -200,34 +231,43 @@
 
 
 def on_device(ny, nz, volume, down_weight, conv_one, conv_two, norm_gain, norm_shift):
-    coarse = strided(volume, down_weight)
-    rows, depth, length, channels = coarse.shape
+    inputs, rows, depth, length = volume.shape
+    rows, depth, length = rows // 2, depth // 2, length // 2
+    channels = down_weight.shape[0]
+    cells = rows * depth * length
+    down = jnp.transpose(down_weight, (1, 2, 3, 4, 0)).reshape(8 * inputs, channels)
     vmem = pl.BlockSpec(memory_space=pltpu.VMEM)
-    hbm = pl.BlockSpec(memory_space=pl.ANY)
+    hbm = pl.BlockSpec(memory_space=pltpu.HBM)
     count = ny * nz
     out = pl.pallas_call(
         functools.partial(kernel, ny, nz),
-        out_shape=jax.ShapeDtypeStruct(coarse.shape, jnp.bfloat16),
-        in_specs=[vmem, hbm, hbm, vmem, vmem],
+        out_shape=jax.ShapeDtypeStruct((rows, depth, length, channels), jnp.bfloat16),
+        in_specs=[hbm, hbm, hbm, hbm, vmem, vmem],
         out_specs=vmem,
         scratch_shapes=[
+            pltpu.VMEM(volume.shape, jnp.bfloat16),
+            pltpu.VMEM(down.shape, jnp.bfloat16),
+            pltpu.VMEM(volume.shape, jnp.float32),
+            pltpu.VMEM(down.shape, jnp.float32),
+            pltpu.VMEM((2, 2 * cells, channels), jnp.float32),
             pltpu.VMEM(conv_one.shape, jnp.bfloat16),
             pltpu.VMEM(conv_two.shape, jnp.bfloat16),
+            pltpu.VMEM((9 * channels, 3 * channels), jnp.bfloat16),
             pltpu.VMEM((3, 2, channels), jnp.float32),
             pltpu.VMEM((3, count - 1, 2, channels), jnp.float32),
             pltpu.VMEM((2, rows, depth, length, channels), jnp.bfloat16),
             pltpu.VMEM((2, rows + 2, depth + 2, length, channels), jnp.bfloat16),
             pltpu.VMEM((rows + 2, depth + 2, length, channels), jnp.bfloat16),
-            pltpu.SemaphoreType.DMA((2,)),
+            pltpu.SemaphoreType.DMA((4,)),
             pltpu.SemaphoreType.DMA((3,)),
             pltpu.SemaphoreType.DMA((3,)),
             pltpu.SemaphoreType.DMA((2, len(SIDES))),
             pltpu.SemaphoreType.DMA((2, len(SIDES))),
         ],
         compiler_params=pltpu.CompilerParams(
-            collective_id=0, has_side_effects=True, vmem_limit_bytes=40 * 1024 * 1024
+            collective_id=0, has_side_effects=True, vmem_limit_bytes=56 * 1024 * 1024
         ),
-    )(coarse, conv_one, conv_two, norm_gain, norm_shift)
+    )(volume, down, conv_one, conv_two, norm_gain, norm_shift)
     return jnp.transpose(out, (3, 0, 1, 2))
 
 

time: 32.1 us -> 27.8 us (0.87)
  local copies, waits for them, and re-layouts: 4.36 us -> 1.68 us
  Pallas kernels: 27.2 us -> 26 us
  matrix products: 0.35 us -> 0 us
    unnamed x11 -> x0, local copies, waits for them, and re-layouts: 3.57 us -> none
    pallas_call x1, Pallas kernels: 27.2 us -> 26 us  [on_device(): pl.pallas_call(functools.partial(kernel, ny, nz), out_shape=jax.ShapeDtyp...]
    transpose x1, local copies, waits for them, and re-layouts: 0.79 us -> 1.68 us  [on_device(): return jnp.transpose(out, (3, 0, 1, 2))]
    dot_general x1 -> x0, matrix products: 0.35 us -> none  [strided(): jnp.einsum('oiabc,iyazbxc->yzxo', down_weight, blocks, preferred_element_...]
where the time goes in v2:
time: 27.8 us; the launch traced here: 27.6 us
  Pallas kernels  26 us (94%)
  local copies, waits for them, and re-layouts  1.68 us (6%)
    pallas_call x1, Pallas kernels, on_device(): pl.pallas_call(functools.partial(kernel, ny, nz), out_shape=jax.ShapeDtyp...  26 us
    transpose x1, local copies, waits for them, and re-layouts, on_device(): return jnp.transpose(out, (3, 0, 1, 2))  1.68 us

profile of v2, /device:TPU:0, one launch (start us, length us, event | category | flops | bytes accessed | tf_op | source)
XLA Modules:
  0.0 27.6 jit_solution(12972450691483241098)
XLA Ops:
  0.0 26.0 %shard_map.64 = bf16[2,2,128,128]{3,2,1,0:T(8,128)(2,1)} custom-call(bf16[64,4,4,256]{3,2,1,0:T(4,128)(2,1)} %volume_hbm.1, bf16[512,128]{1,0:T(8,128)(2,1)} %bitcast.5, bf16[3,3,128,384]{3,2,1,0:T(8,128)(2,1)} %one_hbm.1, bf16[3,3,128,384]{3,2,1,0:T(8,128)(2,1)} %two_hbm.1, f32[3,128]{1,0:T(4,128)} %gain_ref.1, f32[3,128]{1,0:T(4,128)} %shift_ref.1), custom_call_target="tpu_custom_call" | custom-call | tf_op jit(solution)/shard_map/pallas_call | solution.py:242
  26.0 1.7 %copy.7 = bf16[128,2,2,128]{3,2,1,0:T(2,128)(2,1)} copy(bf16[128,2,2,128]{0,3,2,1:T(8,128)(2,1)} %bitcast.4) | data formatting | bytes 262144 | tf_op jit(solution)/shard_map/transpose | solution.py:271
